TPU v7x, 256 devices: a whole 4x4x8 slice. The times are simulated.
256 devices in a mesh: strike: 32 (over z, y_hi, core), cross: 8 (over x, y_lo).
Axes of the slice: x: 4, y: 4 (y_hi: 2, y_lo: 2; y = y_hi * 2 + y_lo), z: 8, core: 2. Of those that a mesh axis runs over, the one named last changes fastest.
Arguments:
- velocity: float32 [3, 512, 128, 256], P(None, 'strike', 'cross'), may hold values from -4 to 4
- stress: float32 [6, 512, 128, 256], P(None, 'strike', 'cross'), may hold values from -1.6 to 1.6
- buoyancy: float32 [512, 128, 256], P('strike', 'cross'), may hold values from 0.5 to 1
- lame: float32 [512, 128, 256], P('strike', 'cross'), may hold values from 0.5 to 1.2
- shear: float32 [512, 128, 256], P('strike', 'cross'), may hold values from 0.5 to 1
- fault_tile: int32 [32], replicated, may hold values from 1 to 7
- prestress: float32 [512, 256], P('strike', 'cross'), may hold values from 1.2 to 2.4
- normal_stress: float32 [512, 256], P('strike', 'cross'), may hold values from 2 to 4
- rate_a: float32 [512, 256], P('strike', 'cross'), may hold values from 0.02 to 0.04
- state: float32 [512, 256], P('strike', 'cross'), may hold values from 0.45 to 0.6
Outputs:
- velocity_out: float32 [3, 512, 128, 256], P(None, 'strike', 'cross')
- stress_out: float32 [6, 512, 128, 256], P(None, 'strike', 'cross')
- slip_rate: float32 [512, 256], P('strike', 'cross')
- state_out: float32 [512, 256], P('strike', 'cross')
Inputs may be any that keep to these rules, and one draw needn't show every extreme that they name: `fault_tile`: each strike index has its fault plane in the first row of one cross tile other than the first.
All inputs are finite; a program needn't handle non-finite values.
Results may differ from a plain program's by a relative error of at most 0.0003.
Values sent between devices are 32-bit elements; how exact they have to be, the bound alone decides.
A program may use at most 64 MiB of HBM per device.

v0:
```python
import jax
import jax.numpy as jnp
from jax import lax
from jax.sharding import PartitionSpec as P

STEPS = 4
NEWTON = 8
step_ratio = 0.25
ref_rate = 0.001
evolve_rate = 1e-05
base_friction = 0.6
evolve_b = 0.03


def with_halo(shard, sides, width):
    for axis, dim in sides:
        size, length = (lax.axis_size(axis), shard.shape[dim])
        up = [(i, (i + 1) % size) for i in range(size - 1)]
        down = [(j, i) for i, j in up]
        last = lax.slice_in_dim(shard, length - width, length, axis=dim)
        first = lax.slice_in_dim(shard, 0, width, axis=dim)
        before = lax.ppermute(last, axis, up)
        after = lax.ppermute(first, axis, down)
        shard = jnp.concatenate([before, shard, after], axis=dim)
    return shard


def inverse_sinh(value):
    magnitude = jnp.abs(value)
    return jnp.sign(value) * jnp.log(magnitude + jnp.sqrt(magnitude * magnitude + 1.0))


def shifted(field, axis_pos, offset):
    parts = [slice(2, field.shape[position] - 2) for position in range(3)]
    parts[axis_pos] = slice(2 + offset, field.shape[axis_pos] - 2 + offset)
    return field[tuple(parts)]


def forward_diff(field, axis_pos):
    return (
        1.125 * (shifted(field, axis_pos, 1) - shifted(field, axis_pos, 0))
        - (shifted(field, axis_pos, 2) - shifted(field, axis_pos, -1)) / 24.0
    )


def backward_diff(field, axis_pos):
    return (
        1.125 * (shifted(field, axis_pos, 0) - shifted(field, axis_pos, -1))
        - (shifted(field, axis_pos, 1) - shifted(field, axis_pos, -2)) / 24.0
    )


def velocity_update(velocity, padded, buoyancy):
    strike_force = (
        forward_diff(padded[0], 0) + backward_diff(padded[3], 1) + backward_diff(padded[4], 2)
    )
    cross_force = (
        backward_diff(padded[3], 0) + forward_diff(padded[1], 1) + backward_diff(padded[5], 2)
    )
    depth_force = (
        backward_diff(padded[4], 0) + backward_diff(padded[5], 1) + forward_diff(padded[2], 2)
    )
    return velocity + step_ratio * buoyancy * jnp.stack([strike_force, cross_force, depth_force])


def stress_update(stress, padded, lame, shear):
    stretch_strike = backward_diff(padded[0], 0)
    stretch_cross = backward_diff(padded[1], 1)
    stretch_depth = backward_diff(padded[2], 2)
    dilation = stretch_strike + stretch_cross + stretch_depth
    normal = jnp.stack(
        [
            lame * dilation + 2.0 * shear * stretch_strike,
            lame * dilation + 2.0 * shear * stretch_cross,
            lame * dilation + 2.0 * shear * stretch_depth,
        ]
    )
    tangent = shear * jnp.stack(
        [
            forward_diff(padded[0], 1) + forward_diff(padded[1], 0),
            forward_diff(padded[0], 2) + forward_diff(padded[2], 0),
            forward_diff(padded[1], 2) + forward_diff(padded[2], 1),
        ]
    )
    return stress + step_ratio * jnp.concatenate([normal, tangent], 0)


def friction(trial, damping, prestress, normal_stress, rate_a, state):
    total = trial + prestress
    width = 2.0 * ref_rate * jnp.exp(-state / rate_a)
    strength = rate_a * normal_stress
    scaled = inverse_sinh(total / (damping * width))
    for iteration in range(NEWTON):
        residual = strength * scaled + damping * width * jnp.sinh(scaled) - total
        slope = strength + damping * width * jnp.cosh(scaled)
        scaled = scaled - residual / slope
    slip = width * jnp.sinh(scaled)
    traction = total - damping * slip
    evolved = state + evolve_rate * (
        jnp.exp((base_friction - state) / evolve_b) - jnp.abs(slip) / ref_rate
    )
    return (traction - prestress, slip, evolved)


def pad_depth(field):
    return jnp.pad(field, ((0, 0), (0, 0), (0, 0), (2, 2)))


def local(
    velocity, stress, buoyancy, lame, shear, fault_tile, prestress, normal_stress, rate_a, state
):
    strike_pos = lax.axis_index("strike")
    cross_pos = lax.axis_index("cross")
    is_owner = fault_tile[strike_pos] == cross_pos
    damping = 0.5 * jnp.sqrt(shear[:, 0, :] / buoyancy[:, 0, :])
    fault_prestress, fault_normal, fault_rate, fault_state = (
        lax.all_gather(prestress, "cross", axis=1, tiled=True),
        lax.all_gather(normal_stress, "cross", axis=1, tiled=True),
        lax.all_gather(rate_a, "cross", axis=1, tiled=True),
        lax.all_gather(state, "cross", axis=1, tiled=True),
    )
    slip = jnp.zeros_like(fault_state)
    for iteration in range(STEPS):
        stress_wide = with_halo(stress, (("strike", 1), ("cross", 2)), 2)
        velocity = velocity_update(velocity, pad_depth(stress_wide), buoyancy)
        velocity_wide = with_halo(velocity, (("strike", 1), ("cross", 2)), 2)
        stress = stress_update(stress, pad_depth(velocity_wide), lame, shear)
        trial = stress[3, :, 0, :]
        change, slip, fault_state = friction(
            trial, damping, fault_prestress, fault_normal, fault_rate, fault_state
        )
        update = jnp.where(is_owner, change, trial)
        stress = stress.at[3, :, 0, :].set(update)
    slip_out, state_out = (
        lax.psum_scatter(jnp.where(is_owner, slip, 0.0), "cross", scatter_dimension=1, tiled=True),
        lax.psum_scatter(
            jnp.where(is_owner, fault_state, 0.0), "cross", scatter_dimension=1, tiled=True
        ),
    )
    return (velocity, stress, slip_out, state_out)


def solution(mesh):
    in_specs = (
        P(None, "strike", "cross", None),
        P(None, "strike", "cross", None),
        P("strike", "cross", None),
        P("strike", "cross", None),
        P("strike", "cross", None),
        P(),
        P("strike", "cross"),
        P("strike", "cross"),
        P("strike", "cross"),
        P("strike", "cross"),
    )
    out_specs = (
        P(None, "strike", "cross", None),
        P(None, "strike", "cross", None),
        P("strike", "cross"),
        P("strike", "cross"),
    )
    return jax.shard_map(local, mesh=mesh, in_specs=in_specs, out_specs=out_specs, check_vma=False)
```

profile of v0, /device:TPU:32, one launch (start us, length us, event | category | flops | bytes accessed | tf_op | source)
XLA Modules:
  0.0 468.4 jit_solution(657342428143192859)
XLA Ops:
  7.2 2.3 copy.51
  9.7 1.9 collective-permute-start
  11.6 6.0 %collective-permute-start.1 = (f32[6,2,16,256]{3,1,2,0:T(2,128)S(1)}, f32[6,2,16,256]{3,1,2,0:T(2,128)S(1)}, u32[]{:S(2)}, u32[]{:S(2)}) collective-permute-start(f32[6,2,16,256]{3,1,2,0:T(2,128)S(1)} %get-tuple-element.137), channel_id=1, source_target_pairs={{8,0},{16,8},{24,16},{32,24},{40,32},{48,40},{56,48},{64,56},{72,6... | collective-permute-start | bytes 589832 | tf_op jit(solution)/shard_map/ppermute | solution.py:23
  17.7 1.4 collective-permute-done
  19.1 1.8 collective-permute-done.1
  20.9 3.5 collective-permute-start.2
  24.5 1.3 collective-permute-start.3
  26.0 11.5 %collective-permute-done.2 = f32[6,20,2,256]{3,1,2,0:T(8,128)S(1)} collective-permute-done((f32[6,20,2,256]{3,1,2,0:T(8,128)S(1)}, f32[6,20,2,256]{3,1,2,0:T(8,128)S(1)}, u32[]{:S(2)}, u32[]{:S(2)}) %collective-permute-start.2) | collective-permute-done | bytes 245792 | tf_op jit(solution)/shard_map/ppermute | solution.py:22
  37.5 3.0 select_maximum_fusion.12
  44.1 2.7 collective-permute-start.4
  46.8 5.3 %collective-permute-start.5 = (f32[3,2,16,256]{3,1,2,0:T(2,128)S(1)}, f32[3,2,16,256]{3,1,2,0:T(2,128)S(1)}, u32[]{:S(2)}, u32[]{:S(2)}) collective-permute-start(f32[3,2,16,256]{3,1,2,0:T(2,128)S(1)} %get-tuple-element.157), channel_id=1, source_target_pairs={{8,0},{16,8},{24,16},{32,24},{40,32},{48,40},{56,48},{64,56},{72,6... | collective-permute-start | bytes 294920 | tf_op jit(solution)/shard_map/ppermute | solution.py:23
  52.5 1.8 collective-permute-done.5
  54.3 4.4 collective-permute-start.6
  58.7 1.3 collective-permute-start.7
  60.1 31.8 %all-gather = f32[8,32,16]{1,2,0:T(8,128)S(1)} all-gather(f32[1,32,16]{1,2,0:T(8,128)S(1)} %bitcast.312), channel_id=1, replica_groups=mesh['strike'=32,'cross'=8] {'cross'}, dimensions={0}, use_global_device_ids=true | all-gather | bytes 18432 | tf_op jit(solution)/shard_map/all_gather | solution.py:117
  92.0 28.2 %all-gather.3 = f32[8,32,16]{1,2,0:T(8,128)S(1)} all-gather(f32[1,32,16]{1,2,0:T(8,128)S(1)} %bitcast.313), channel_id=1, replica_groups=mesh['strike'=32,'cross'=8] {'cross'}, dimensions={0}, use_global_device_ids=true | all-gather | bytes 18432 | tf_op jit(solution)/shard_map/all_gather | solution.py:118
  120.2 28.2 %all-gather.2 = f32[8,32,16]{1,2,0:T(8,128)S(1)} all-gather(f32[1,32,16]{1,2,0:T(8,128)S(1)} %bitcast.314), channel_id=1, replica_groups=mesh['strike'=32,'cross'=8] {'cross'}, dimensions={0}, use_global_device_ids=true | all-gather | bytes 18432 | tf_op jit(solution)/shard_map/all_gather | solution.py:119
  148.5 28.3 %all-gather.1 = f32[8,32,16]{1,2,0:T(8,128)S(1)} all-gather(f32[1,32,16]{1,2,0:T(8,128)S(1)} %bitcast.315), channel_id=1, replica_groups=mesh['strike'=32,'cross'=8] {'cross'}, dimensions={0}, use_global_device_ids=true | all-gather | bytes 18432 | tf_op jit(solution)/shard_map/all_gather | solution.py:120
  185.6 1.9 collective-permute-start.8
  187.5 6.0 %collective-permute-start.9 = (f32[6,2,16,256]{3,1,2,0:T(2,128)S(1)}, f32[6,2,16,256]{3,1,2,0:T(2,128)S(1)}, u32[]{:S(2)}, u32[]{:S(2)}) collective-permute-start(f32[6,2,16,256]{3,1,2,0:T(2,128)S(1)} %get-tuple-element.135), channel_id=1, source_target_pairs={{8,0},{16,8},{24,16},{32,24},{40,32},{48,40},{56,48},{64,56},{72,6... | collective-permute-start | bytes 589832 | tf_op jit(solution)/shard_map/ppermute | solution.py:23
  193.6 1.4 collective-permute-done.8
  195.0 1.8 collective-permute-done.9
  196.9 1.3 collective-permute-start.10
  198.2 1.3 collective-permute-start.11
  199.5 12.4 %collective-permute-done.10 = f32[6,20,2,256]{3,1,2,0:T(8,128)S(1)} collective-permute-done((f32[6,20,2,256]{3,1,2,0:T(8,128)S(1)}, f32[6,20,2,256]{3,1,2,0:T(8,128)S(1)}, u32[]{:S(2)}, u32[]{:S(2)}) %collective-permute-start.10) | collective-permute-done | bytes 245792 | tf_op jit(solution)/shard_map/ppermute | solution.py:22
  211.9 3.0 select_maximum_fusion.8
  218.3 1.9 collective-permute-start.12
  220.3 6.0 %collective-permute-start.13 = (f32[3,2,16,256]{3,1,2,0:T(2,128)S(1)}, f32[3,2,16,256]{3,1,2,0:T(2,128)S(1)}, u32[]{:S(2)}, u32[]{:S(2)}) collective-permute-start(f32[3,2,16,256]{3,1,2,0:T(2,128)S(1)} %get-tuple-element.155), channel_id=1, source_target_pairs={{8,0},{16,8},{24,16},{32,24},{40,32},{48,40},{56,48},{64,56},{72,6... | collective-permute-start | bytes 294920 | tf_op jit(solution)/shard_map/ppermute | solution.py:23
  226.7 1.8 collective-permute-done.13
  228.6 4.4 collective-permute-start.14
  232.9 1.5 collective-permute-start.15
  235.6 4.4 collective-permute-done.15
  244.8 1.9 collective-permute-start.16
  246.7 6.0 %collective-permute-start.17 = (f32[6,2,16,256]{3,1,2,0:T(2,128)S(1)}, f32[6,2,16,256]{3,1,2,0:T(2,128)S(1)}, u32[]{:S(2)}, u32[]{:S(2)}) collective-permute-start(f32[6,2,16,256]{3,1,2,0:T(2,128)S(1)} %get-tuple-element.133), channel_id=1, source_target_pairs={{8,0},{16,8},{24,16},{32,24},{40,32},{48,40},{56,48},{64,56},{72,6... | collective-permute-start | bytes 589832 | tf_op jit(solution)/shard_map/ppermute | solution.py:23
  252.8 1.4 collective-permute-done.16
  254.2 1.8 collective-permute-done.17
  256.1 4.8 %collective-permute-start.18 = (f32[6,20,2,256]{3,1,2,0:T(8,128)S(1)}, f32[6,20,2,256]{3,1,2,0:T(8,128)S(1)}, u32[]{:S(2)}, u32[]{:S(2)}) collective-permute-start(f32[6,20,2,256]{3,1,2,0:T(8,128)S(1)} %get-tuple-element.124), channel_id=1, source_target_pairs={{0,1},{1,2},{2,3},{3,4},{4,5},{5,6},{6,7},{8,9},{9,10},{10,11},{11... | collective-permute-start | bytes 737288 | tf_op jit(solution)/shard_map/ppermute | solution.py:22
  262.2 11.6 %collective-permute-done.18 = f32[6,20,2,256]{3,1,2,0:T(8,128)S(1)} collective-permute-done((f32[6,20,2,256]{3,1,2,0:T(8,128)S(1)}, f32[6,20,2,256]{3,1,2,0:T(8,128)S(1)}, u32[]{:S(2)}, u32[]{:S(2)}) %collective-permute-start.18) | collective-permute-done | bytes 245792 | tf_op jit(solution)/shard_map/ppermute | solution.py:22
  273.7 3.0 select_maximum_fusion.4
  280.3 1.9 collective-permute-start.20
  282.3 6.0 %collective-permute-start.21 = (f32[3,2,16,256]{3,1,2,0:T(2,128)S(1)}, f32[3,2,16,256]{3,1,2,0:T(2,128)S(1)}, u32[]{:S(2)}, u32[]{:S(2)}) collective-permute-start(f32[3,2,16,256]{3,1,2,0:T(2,128)S(1)} %get-tuple-element.153), channel_id=1, source_target_pairs={{8,0},{16,8},{24,16},{32,24},{40,32},{48,40},{56,48},{64,56},{72,6... | collective-permute-start | bytes 294920 | tf_op jit(solution)/shard_map/ppermute | solution.py:23
  288.7 1.8 collective-permute-done.21
  290.6 4.4 collective-permute-start.22
  295.0 1.7 collective-permute-start.23
  297.6 4.4 collective-permute-done.23
  306.8 1.9 collective-permute-start.24
  308.7 6.0 %collective-permute-start.25 = (f32[6,2,16,256]{3,1,2,0:T(2,128)S(1)}, f32[6,2,16,256]{3,1,2,0:T(2,128)S(1)}, u32[]{:S(2)}, u32[]{:S(2)}) collective-permute-start(f32[6,2,16,256]{3,1,2,0:T(2,128)S(1)} %get-tuple-element.131), channel_id=1, source_target_pairs={{8,0},{16,8},{24,16},{32,24},{40,32},{48,40},{56,48},{64,56},{72,6... | collective-permute-start | bytes 589832 | tf_op jit(solution)/shard_map/ppermute | solution.py:23
  314.8 1.4 collective-permute-done.24
  316.2 1.8 collective-permute-done.25
  318.1 4.8 %collective-permute-start.26 = (f32[6,20,2,256]{3,1,2,0:T(8,128)S(1)}, f32[6,20,2,256]{3,1,2,0:T(8,128)S(1)}, u32[]{:S(2)}, u32[]{:S(2)}) collective-permute-start(f32[6,20,2,256]{3,1,2,0:T(8,128)S(1)} %get-tuple-element.122), channel_id=1, source_target_pairs={{0,1},{1,2},{2,3},{3,4},{4,5},{5,6},{6,7},{8,9},{9,10},{10,11},{11... | collective-permute-start | bytes 737288 | tf_op jit(solution)/shard_map/ppermute | solution.py:22
  324.2 11.6 %collective-permute-done.26 = f32[6,20,2,256]{3,1,2,0:T(8,128)S(1)} collective-permute-done((f32[6,20,2,256]{3,1,2,0:T(8,128)S(1)}, f32[6,20,2,256]{3,1,2,0:T(8,128)S(1)}, u32[]{:S(2)}, u32[]{:S(2)}) %collective-permute-start.26) | collective-permute-done | bytes 245792 | tf_op jit(solution)/shard_map/ppermute | solution.py:22
  335.8 3.0 select_maximum_fusion
  342.4 1.9 collective-permute-start.28
  344.3 6.0 %collective-permute-start.29 = (f32[3,2,16,256]{3,1,2,0:T(2,128)S(1)}, f32[3,2,16,256]{3,1,2,0:T(2,128)S(1)}, u32[]{:S(2)}, u32[]{:S(2)}) collective-permute-start(f32[3,2,16,256]{3,1,2,0:T(2,128)S(1)} %get-tuple-element.151), channel_id=1, source_target_pairs={{8,0},{16,8},{24,16},{32,24},{40,32},{48,40},{56,48},{64,56},{72,6... | collective-permute-start | bytes 294920 | tf_op jit(solution)/shard_map/ppermute | solution.py:23
  350.8 1.8 collective-permute-done.29
  352.6 4.4 collective-permute-start.30
  357.0 1.5 collective-permute-start.31
  358.5 1.3 copy.68
  359.8 4.2 collective-permute-done.31
  370.3 2.0 copy.69
  372.4 46.8 %reduce-scatter.7.cloned.1.call-done = f32[32,16]{1,0:T(8,128)} async-done(((f32[256,16]{1,0:T(8,128)}), f32[32,16]{1,0:T(8,128)}) %reduce-scatter.7.cloned.1.call-update) | async-done | bytes 2064
  419.2 1.4 copy.71
  420.6 39.4 %reduce-scatter.9.cloned.1.call-done = f32[32,16]{1,0:T(8,128)} async-done(((f32[256,16]{1,0:T(8,128)}), f32[32,16]{1,0:T(8,128)}) %reduce-scatter.9.cloned.1.call-update) | async-done | bytes 2064
  460.0 1.4 copy.73
  (132 shorter events, 45.4 us)
Async XLA Ops:
  7.2 412.0 %reduce-scatter.7.cloned.1.call-start = ((), (), s32[]{:S(2)}) async-start(), calls=%async_computation.2 | async-start | bytes 147456
  9.5 16.2 %copy-start.4 = (f32[16,16,256]{2,1,0:T(8,128)S(1)}, f32[16,16,256]{2,1,0:T(8,128)}, u32[]{:S(2)}) copy-start(f32[16,16,256]{2,1,0:T(8,128)} %param.20) | copy-start | bytes 786436
  9.7 9.4 %collective-permute-start = (f32[6,2,16,256]{3,1,2,0:T(2,128)S(1)}, f32[6,2,16,256]{3,1,2,0:T(2,128)S(1)}, u32[]{:S(2)}, u32[]{:S(2)}) collective-permute-start(f32[6,2,16,256]{3,1,2,0:T(2,128)S(1)} %get-tuple-element.136), channel_id=1, source_target_pairs={{0,8},{8,16},{16,24},{24,32},{32,40},{40,48},{48,56},{56,64},{64,7... | collective-permute-start | bytes 589832 | tf_op jit(solution)/shard_map/ppermute | solution.py:22
  11.6 9.2 %collective-permute-start.1 = (f32[6,2,16,256]{3,1,2,0:T(2,128)S(1)}, f32[6,2,16,256]{3,1,2,0:T(2,128)S(1)}, u32[]{:S(2)}, u32[]{:S(2)}) collective-permute-start(f32[6,2,16,256]{3,1,2,0:T(2,128)S(1)} %get-tuple-element.137), channel_id=1, source_target_pairs={{8,0},{16,8},{24,16},{32,24},{40,32},{48,40},{56,48},{64,56},{72,6... | collective-permute-start | bytes 589832 | tf_op jit(solution)/shard_map/ppermute | solution.py:23
  20.9 16.5 %collective-permute-start.2 = (f32[6,20,2,256]{3,1,2,0:T(8,128)S(1)}, f32[6,20,2,256]{3,1,2,0:T(8,128)S(1)}, u32[]{:S(2)}, u32[]{:S(2)}) collective-permute-start(f32[6,20,2,256]{3,1,2,0:T(8,128)S(1)} %get-tuple-element.128), channel_id=1, source_target_pairs={{0,1},{1,2},{2,3},{3,4},{4,5},{5,6},{6,7},{8,9},{9,10},{10,11},{11... | collective-permute-start | bytes 737288 | tf_op jit(solution)/shard_map/ppermute | solution.py:22
  24.5 13.0 %collective-permute-start.3 = (f32[6,20,2,256]{3,1,2,0:T(8,128)S(1)}, f32[6,20,2,256]{3,1,2,0:T(8,128)S(1)}, u32[]{:S(2)}, u32[]{:S(2)}) collective-permute-start(f32[6,20,2,256]{3,1,2,0:T(8,128)S(1)} %get-tuple-element.129), channel_id=1, source_target_pairs={{1,0},{2,1},{3,2},{4,3},{5,4},{6,5},{7,6},{9,8},{10,9},{11,10},{12... | collective-permute-start | bytes 737288 | tf_op jit(solution)/shard_map/ppermute | solution.py:23
  42.4 1.1 copy-start.1
  43.5 16.6 %copy-start.5 = (f32[16,32]{1,0:T(8,128)S(1)}, f32[16,32]{1,0:T(8,128)}, u32[]{:S(2)}) copy-start(f32[16,32]{1,0:T(8,128)} %param.24) | copy-start | bytes 6148
  43.5 48.4 %copy-start.6 = (f32[16,32]{1,0:T(8,128)S(1)}, f32[16,32]{1,0:T(8,128)}, u32[]{:S(2)}) copy-start(f32[16,32]{1,0:T(8,128)} %param.25) | copy-start | bytes 6148
  43.5 76.7 %copy-start.7 = (f32[16,32]{1,0:T(8,128)S(1)}, f32[16,32]{1,0:T(8,128)}, u32[]{:S(2)}) copy-start(f32[16,32]{1,0:T(8,128)} %param.26) | copy-start | bytes 6148
  43.5 105.0 %copy-start.8 = (f32[16,32]{1,0:T(8,128)S(1)}, f32[16,32]{1,0:T(8,128)}, u32[]{:S(2)}) copy-start(f32[16,32]{1,0:T(8,128)} %param.27) | copy-start | bytes 6148
  44.1 8.3 %collective-permute-start.4 = (f32[3,2,16,256]{3,1,2,0:T(2,128)S(1)}, f32[3,2,16,256]{3,1,2,0:T(2,128)S(1)}, u32[]{:S(2)}, u32[]{:S(2)}) collective-permute-start(f32[3,2,16,256]{3,1,2,0:T(2,128)S(1)} %get-tuple-element.156), channel_id=1, source_target_pairs={{0,8},{8,16},{16,24},{24,32},{32,40},{40,48},{48,56},{56,64},{64,7... | collective-permute-start | bytes 294920 | tf_op jit(solution)/shard_map/ppermute | solution.py:22
  46.8 7.5 %collective-permute-start.5 = (f32[3,2,16,256]{3,1,2,0:T(2,128)S(1)}, f32[3,2,16,256]{3,1,2,0:T(2,128)S(1)}, u32[]{:S(2)}, u32[]{:S(2)}) collective-permute-start(f32[3,2,16,256]{3,1,2,0:T(2,128)S(1)} %get-tuple-element.157), channel_id=1, source_target_pairs={{8,0},{16,8},{24,16},{32,24},{40,32},{48,40},{56,48},{64,56},{72,6... | collective-permute-start | bytes 294920 | tf_op jit(solution)/shard_map/ppermute | solution.py:23
  54.3 124.5 %collective-permute-start.6 = (f32[3,20,2,256]{3,1,2,0:T(8,128)S(1)}, f32[3,20,2,256]{3,1,2,0:T(8,128)S(1)}, u32[]{:S(2)}, u32[]{:S(2)}) collective-permute-start(f32[3,20,2,256]{3,1,2,0:T(8,128)S(1)} %get-tuple-element.148), channel_id=1, source_target_pairs={{0,1},{1,2},{2,3},{3,4},{4,5},{5,6},{6,7},{8,9},{9,10},{10,11},{11... | collective-permute-start | bytes 368648 | tf_op jit(solution)/shard_map/ppermute | solution.py:22
  58.7 120.1 %collective-permute-start.7 = (f32[3,20,2,256]{3,1,2,0:T(8,128)S(1)}, f32[3,20,2,256]{3,1,2,0:T(8,128)S(1)}, u32[]{:S(2)}, u32[]{:S(2)}) collective-permute-start(f32[3,20,2,256]{3,1,2,0:T(8,128)S(1)} %get-tuple-element.149), channel_id=1, source_target_pairs={{1,0},{2,1},{3,2},{4,3},{5,4},{6,5},{7,6},{9,8},{10,9},{11,10},{12... | collective-permute-start | bytes 368648 | tf_op jit(solution)/shard_map/ppermute | solution.py:23
  180.7 1.0 copy-start
  180.7 1.0 copy-start.3
  182.7 1.4 copy-start.2
  185.6 9.4 %collective-permute-start.8 = (f32[6,2,16,256]{3,1,2,0:T(2,128)S(1)}, f32[6,2,16,256]{3,1,2,0:T(2,128)S(1)}, u32[]{:S(2)}, u32[]{:S(2)}) collective-permute-start(f32[6,2,16,256]{3,1,2,0:T(2,128)S(1)} %get-tuple-element.134), channel_id=1, source_target_pairs={{0,8},{8,16},{16,24},{24,32},{32,40},{40,48},{48,56},{56,64},{64,7... | collective-permute-start | bytes 589832 | tf_op jit(solution)/shard_map/ppermute | solution.py:22
  187.5 9.3 %collective-permute-start.9 = (f32[6,2,16,256]{3,1,2,0:T(2,128)S(1)}, f32[6,2,16,256]{3,1,2,0:T(2,128)S(1)}, u32[]{:S(2)}, u32[]{:S(2)}) collective-permute-start(f32[6,2,16,256]{3,1,2,0:T(2,128)S(1)} %get-tuple-element.135), channel_id=1, source_target_pairs={{8,0},{16,8},{24,16},{32,24},{40,32},{48,40},{56,48},{64,56},{72,6... | collective-permute-start | bytes 589832 | tf_op jit(solution)/shard_map/ppermute | solution.py:23
  196.9 15.0 %collective-permute-start.10 = (f32[6,20,2,256]{3,1,2,0:T(8,128)S(1)}, f32[6,20,2,256]{3,1,2,0:T(8,128)S(1)}, u32[]{:S(2)}, u32[]{:S(2)}) collective-permute-start(f32[6,20,2,256]{3,1,2,0:T(8,128)S(1)} %get-tuple-element.126), channel_id=1, source_target_pairs={{0,1},{1,2},{2,3},{3,4},{4,5},{5,6},{6,7},{8,9},{9,10},{10,11},{11... | collective-permute-start | bytes 737288 | tf_op jit(solution)/shard_map/ppermute | solution.py:22
  198.2 13.7 %collective-permute-start.11 = (f32[6,20,2,256]{3,1,2,0:T(8,128)S(1)}, f32[6,20,2,256]{3,1,2,0:T(8,128)S(1)}, u32[]{:S(2)}, u32[]{:S(2)}) collective-permute-start(f32[6,20,2,256]{3,1,2,0:T(8,128)S(1)} %get-tuple-element.127), channel_id=1, source_target_pairs={{1,0},{2,1},{3,2},{4,3},{5,4},{6,5},{7,6},{9,8},{10,9},{11,10},{12... | collective-permute-start | bytes 737288 | tf_op jit(solution)/shard_map/ppermute | solution.py:23
  218.3 8.3 %collective-permute-start.12 = (f32[3,2,16,256]{3,1,2,0:T(2,128)S(1)}, f32[3,2,16,256]{3,1,2,0:T(2,128)S(1)}, u32[]{:S(2)}, u32[]{:S(2)}) collective-permute-start(f32[3,2,16,256]{3,1,2,0:T(2,128)S(1)} %get-tuple-element.154), channel_id=1, source_target_pairs={{0,8},{8,16},{16,24},{24,32},{32,40},{40,48},{48,56},{56,64},{64,7... | collective-permute-start | bytes 294920 | tf_op jit(solution)/shard_map/ppermute | solution.py:22
  220.3 8.2 %collective-permute-start.13 = (f32[3,2,16,256]{3,1,2,0:T(2,128)S(1)}, f32[3,2,16,256]{3,1,2,0:T(2,128)S(1)}, u32[]{:S(2)}, u32[]{:S(2)}) collective-permute-start(f32[3,2,16,256]{3,1,2,0:T(2,128)S(1)} %get-tuple-element.155), channel_id=1, source_target_pairs={{8,0},{16,8},{24,16},{32,24},{40,32},{48,40},{56,48},{64,56},{72,6... | collective-permute-start | bytes 294920 | tf_op jit(solution)/shard_map/ppermute | solution.py:23
  228.6 7.0 %collective-permute-start.14 = (f32[3,20,2,256]{3,1,2,0:T(8,128)S(1)}, f32[3,20,2,256]{3,1,2,0:T(8,128)S(1)}, u32[]{:S(2)}, u32[]{:S(2)}) collective-permute-start(f32[3,20,2,256]{3,1,2,0:T(8,128)S(1)} %get-tuple-element.146), channel_id=1, source_target_pairs={{0,1},{1,2},{2,3},{3,4},{4,5},{5,6},{6,7},{8,9},{9,10},{10,11},{11... | collective-permute-start | bytes 368648 | tf_op jit(solution)/shard_map/ppermute | solution.py:22
  232.9 7.1 %collective-permute-start.15 = (f32[3,20,2,256]{3,1,2,0:T(8,128)S(1)}, f32[3,20,2,256]{3,1,2,0:T(8,128)S(1)}, u32[]{:S(2)}, u32[]{:S(2)}) collective-permute-start(f32[3,20,2,256]{3,1,2,0:T(8,128)S(1)} %get-tuple-element.147), channel_id=1, source_target_pairs={{1,0},{2,1},{3,2},{4,3},{5,4},{6,5},{7,6},{9,8},{10,9},{11,10},{12... | collective-permute-start | bytes 368648 | tf_op jit(solution)/shard_map/ppermute | solution.py:23
  244.8 9.4 %collective-permute-start.16 = (f32[6,2,16,256]{3,1,2,0:T(2,128)S(1)}, f32[6,2,16,256]{3,1,2,0:T(2,128)S(1)}, u32[]{:S(2)}, u32[]{:S(2)}) collective-permute-start(f32[6,2,16,256]{3,1,2,0:T(2,128)S(1)} %get-tuple-element.132), channel_id=1, source_target_pairs={{0,8},{8,16},{16,24},{24,32},{32,40},{40,48},{48,56},{56,64},{64,7... | collective-permute-start | bytes 589832 | tf_op jit(solution)/shard_map/ppermute | solution.py:22
  246.7 9.3 %collective-permute-start.17 = (f32[6,2,16,256]{3,1,2,0:T(2,128)S(1)}, f32[6,2,16,256]{3,1,2,0:T(2,128)S(1)}, u32[]{:S(2)}, u32[]{:S(2)}) collective-permute-start(f32[6,2,16,256]{3,1,2,0:T(2,128)S(1)} %get-tuple-element.133), channel_id=1, source_target_pairs={{8,0},{16,8},{24,16},{32,24},{40,32},{48,40},{56,48},{64,56},{72,6... | collective-permute-start | bytes 589832 | tf_op jit(solution)/shard_map/ppermute | solution.py:23
  256.1 17.7 %collective-permute-start.18 = (f32[6,20,2,256]{3,1,2,0:T(8,128)S(1)}, f32[6,20,2,256]{3,1,2,0:T(8,128)S(1)}, u32[]{:S(2)}, u32[]{:S(2)}) collective-permute-start(f32[6,20,2,256]{3,1,2,0:T(8,128)S(1)} %get-tuple-element.124), channel_id=1, source_target_pairs={{0,1},{1,2},{2,3},{3,4},{4,5},{5,6},{6,7},{8,9},{9,10},{10,11},{11... | collective-permute-start | bytes 737288 | tf_op jit(solution)/shard_map/ppermute | solution.py:22
  260.9 12.9 %collective-permute-start.19 = (f32[6,20,2,256]{3,1,2,0:T(8,128)S(1)}, f32[6,20,2,256]{3,1,2,0:T(8,128)S(1)}, u32[]{:S(2)}, u32[]{:S(2)}) collective-permute-start(f32[6,20,2,256]{3,1,2,0:T(8,128)S(1)} %get-tuple-element.125), channel_id=1, source_target_pairs={{1,0},{2,1},{3,2},{4,3},{5,4},{6,5},{7,6},{9,8},{10,9},{11,10},{12... | collective-permute-start | bytes 737288 | tf_op jit(solution)/shard_map/ppermute | solution.py:23
  280.3 8.4 %collective-permute-start.20 = (f32[3,2,16,256]{3,1,2,0:T(2,128)S(1)}, f32[3,2,16,256]{3,1,2,0:T(2,128)S(1)}, u32[]{:S(2)}, u32[]{:S(2)}) collective-permute-start(f32[3,2,16,256]{3,1,2,0:T(2,128)S(1)} %get-tuple-element.152), channel_id=1, source_target_pairs={{0,8},{8,16},{16,24},{24,32},{32,40},{40,48},{48,56},{56,64},{64,7... | collective-permute-start | bytes 294920 | tf_op jit(solution)/shard_map/ppermute | solution.py:22
  282.3 8.2 %collective-permute-start.21 = (f32[3,2,16,256]{3,1,2,0:T(2,128)S(1)}, f32[3,2,16,256]{3,1,2,0:T(2,128)S(1)}, u32[]{:S(2)}, u32[]{:S(2)}) collective-permute-start(f32[3,2,16,256]{3,1,2,0:T(2,128)S(1)} %get-tuple-element.153), channel_id=1, source_target_pairs={{8,0},{16,8},{24,16},{32,24},{40,32},{48,40},{56,48},{64,56},{72,6... | collective-permute-start | bytes 294920 | tf_op jit(solution)/shard_map/ppermute | solution.py:23
  290.6 7.1 %collective-permute-start.22 = (f32[3,20,2,256]{3,1,2,0:T(8,128)S(1)}, f32[3,20,2,256]{3,1,2,0:T(8,128)S(1)}, u32[]{:S(2)}, u32[]{:S(2)}) collective-permute-start(f32[3,20,2,256]{3,1,2,0:T(8,128)S(1)} %get-tuple-element.144), channel_id=1, source_target_pairs={{0,1},{1,2},{2,3},{3,4},{4,5},{5,6},{6,7},{8,9},{9,10},{10,11},{11... | collective-permute-start | bytes 368648 | tf_op jit(solution)/shard_map/ppermute | solution.py:22
  295.0 7.0 %collective-permute-start.23 = (f32[3,20,2,256]{3,1,2,0:T(8,128)S(1)}, f32[3,20,2,256]{3,1,2,0:T(8,128)S(1)}, u32[]{:S(2)}, u32[]{:S(2)}) collective-permute-start(f32[3,20,2,256]{3,1,2,0:T(8,128)S(1)} %get-tuple-element.145), channel_id=1, source_target_pairs={{1,0},{2,1},{3,2},{4,3},{5,4},{6,5},{7,6},{9,8},{10,9},{11,10},{12... | collective-permute-start | bytes 368648 | tf_op jit(solution)/shard_map/ppermute | solution.py:23
  306.8 9.4 %collective-permute-start.24 = (f32[6,2,16,256]{3,1,2,0:T(2,128)S(1)}, f32[6,2,16,256]{3,1,2,0:T(2,128)S(1)}, u32[]{:S(2)}, u32[]{:S(2)}) collective-permute-start(f32[6,2,16,256]{3,1,2,0:T(2,128)S(1)} %get-tuple-element.130), channel_id=1, source_target_pairs={{0,8},{8,16},{16,24},{24,32},{32,40},{40,48},{48,56},{56,64},{64,7... | collective-permute-start | bytes 589832 | tf_op jit(solution)/shard_map/ppermute | solution.py:22
  308.7 9.3 %collective-permute-start.25 = (f32[6,2,16,256]{3,1,2,0:T(2,128)S(1)}, f32[6,2,16,256]{3,1,2,0:T(2,128)S(1)}, u32[]{:S(2)}, u32[]{:S(2)}) collective-permute-start(f32[6,2,16,256]{3,1,2,0:T(2,128)S(1)} %get-tuple-element.131), channel_id=1, source_target_pairs={{8,0},{16,8},{24,16},{32,24},{40,32},{48,40},{56,48},{64,56},{72,6... | collective-permute-start | bytes 589832 | tf_op jit(solution)/shard_map/ppermute | solution.py:23
  318.1 17.7 %collective-permute-start.26 = (f32[6,20,2,256]{3,1,2,0:T(8,128)S(1)}, f32[6,20,2,256]{3,1,2,0:T(8,128)S(1)}, u32[]{:S(2)}, u32[]{:S(2)}) collective-permute-start(f32[6,20,2,256]{3,1,2,0:T(8,128)S(1)} %get-tuple-element.122), channel_id=1, source_target_pairs={{0,1},{1,2},{2,3},{3,4},{4,5},{5,6},{6,7},{8,9},{9,10},{10,11},{11... | collective-permute-start | bytes 737288 | tf_op jit(solution)/shard_map/ppermute | solution.py:22
  322.9 12.9 %collective-permute-start.27 = (f32[6,20,2,256]{3,1,2,0:T(8,128)S(1)}, f32[6,20,2,256]{3,1,2,0:T(8,128)S(1)}, u32[]{:S(2)}, u32[]{:S(2)}) collective-permute-start(f32[6,20,2,256]{3,1,2,0:T(8,128)S(1)} %get-tuple-element.123), channel_id=1, source_target_pairs={{1,0},{2,1},{3,2},{4,3},{5,4},{6,5},{7,6},{9,8},{10,9},{11,10},{12... | collective-permute-start | bytes 737288 | tf_op jit(solution)/shard_map/ppermute | solution.py:23
  342.4 8.4 %collective-permute-start.28 = (f32[3,2,16,256]{3,1,2,0:T(2,128)S(1)}, f32[3,2,16,256]{3,1,2,0:T(2,128)S(1)}, u32[]{:S(2)}, u32[]{:S(2)}) collective-permute-start(f32[3,2,16,256]{3,1,2,0:T(2,128)S(1)} %get-tuple-element.150), channel_id=1, source_target_pairs={{0,8},{8,16},{16,24},{24,32},{32,40},{40,48},{48,56},{56,64},{64,7... | collective-permute-start | bytes 294920 | tf_op jit(solution)/shard_map/ppermute | solution.py:22
  344.3 8.2 %collective-permute-start.29 = (f32[3,2,16,256]{3,1,2,0:T(2,128)S(1)}, f32[3,2,16,256]{3,1,2,0:T(2,128)S(1)}, u32[]{:S(2)}, u32[]{:S(2)}) collective-permute-start(f32[3,2,16,256]{3,1,2,0:T(2,128)S(1)} %get-tuple-element.151), channel_id=1, source_target_pairs={{8,0},{16,8},{24,16},{32,24},{40,32},{48,40},{56,48},{64,56},{72,6... | collective-permute-start | bytes 294920 | tf_op jit(solution)/shard_map/ppermute | solution.py:23
  352.6 7.2 %collective-permute-start.30 = (f32[3,20,2,256]{3,1,2,0:T(8,128)S(1)}, f32[3,20,2,256]{3,1,2,0:T(8,128)S(1)}, u32[]{:S(2)}, u32[]{:S(2)}) collective-permute-start(f32[3,20,2,256]{3,1,2,0:T(8,128)S(1)} %get-tuple-element.142), channel_id=1, source_target_pairs={{0,1},{1,2},{2,3},{3,4},{4,5},{5,6},{6,7},{8,9},{9,10},{10,11},{11... | collective-permute-start | bytes 368648 | tf_op jit(solution)/shard_map/ppermute | solution.py:22
  357.0 7.0 %collective-permute-start.31 = (f32[3,20,2,256]{3,1,2,0:T(8,128)S(1)}, f32[3,20,2,256]{3,1,2,0:T(8,128)S(1)}, u32[]{:S(2)}, u32[]{:S(2)}) collective-permute-start(f32[3,20,2,256]{3,1,2,0:T(8,128)S(1)} %get-tuple-element.143), channel_id=1, source_target_pairs={{1,0},{2,1},{3,2},{4,3},{5,4},{6,5},{7,6},{9,8},{10,9},{11,10},{12... | collective-permute-start | bytes 368648 | tf_op jit(solution)/shard_map/ppermute | solution.py:23
  369.5 90.5 %reduce-scatter.9.cloned.1.call-start = ((), (), s32[]{:S(2)}) async-start(), calls=%async_computation.3 | async-start | bytes 147456
Sparse Core Ops, SparseCore 0:
  369.6 49.5 reduce-scatter.6
  421.9 38.0 reduce-scatter.8
where the time goes:
time: 475 us; the launch traced here: 468 us
  waiting for transfers between devices  170 us (36%)
  blocking collectives  116 us (24%)
  starting transfers between devices  107 us (23%)
  other arithmetic  43.4 us (9%)
  local copies, waits for them, and re-layouts  16 us (3%)
  between operations  15.8 us (3%)
    unnamed x4, waiting for transfers between devices  86.3 us
    ppermute x16, starting transfers between devices, with_halo(): after = lax.ppermute(first, axis, down)  58.7 us
    ppermute x16, waiting for transfers between devices, with_halo(): before = lax.ppermute(last, axis, up)  56.3 us
    ppermute x16, starting transfers between devices, with_halo(): before = lax.ppermute(last, axis, up)  48.1 us
    all_gather x1, blocking collectives, local(): lax.all_gather(prestress, 'cross', axis=1, tiled=True)  31.8 us
    all_gather x1, blocking collectives, local(): lax.all_gather(state, 'cross', axis=1, tiled=True)  28.3 us
    all_gather x1, blocking collectives, local(): lax.all_gather(normal_stress, 'cross', axis=1, tiled=True)  28.2 us
    all_gather x1, blocking collectives, local(): lax.all_gather(rate_a, 'cross', axis=1, tiled=True)  28.2 us
  transfers between devices with their start and end apart: 34, of which 27 were waited for; matrix products, arithmetic and copies ran while one was open for 2% of the time, Pallas kernels for 0%

commit v1 on v0

--- a/solution.py
+++ b/solution.py
@@ -117,7 +117,9 @@
         lax.all_gather(prestress, "cross", axis=1, tiled=True),
         lax.all_gather(normal_stress, "cross", axis=1, tiled=True),
         lax.all_gather(rate_a, "cross", axis=1, tiled=True),
-        lax.all_gather(state, "cross", axis=1, tiled=True),
+        jnp.concatenate(
+            lax.all_to_all(jnp.stack([state] * lax.axis_size("cross")), "cross", 0, 0), axis=1
+        ),
     )
     slip = jnp.zeros_like(fault_state)
     for iteration in range(STEPS):

time: 475 us -> 454 us (0.956)
  blocking collectives: 116 us -> 85.1 us
  starting transfers between devices: 107 us -> 116 us
    all_gather x1 -> x0, blocking collectives: 28.3 us -> none  [local(): lax.all_gather(state, 'cross', axis=1, tiled=True)]
    all_to_all x0 -> x1, starting transfers between devices: none -> 7.13 us  [local(): lax.all_to_all(jnp.stack([state] * lax.axis_size('cross')), 'cross', 0, 0)]
    unnamed x29 -> x32, local copies, waits for them, and re-layouts: 11.9 us -> 12.6 us
  transfers between devices with their start and end apart: 34 -> 35, of which waited for: 27 -> 27; matrix products, arithmetic and copies ran while one was open for 2% -> 2% of each run, Pallas kernels for 0% -> 0%
where the time goes in v1:
time: 454 us; the launch traced here: 447 us
  waiting for transfers between devices  169 us (37%)
  starting transfers between devices  116 us (26%)
  blocking collectives  85.1 us (19%)
  other arithmetic  45.1 us (10%)
  local copies, waits for them, and re-layouts  16.6 us (4%)
  between operations  15.9 us (4%)
    unnamed x4, waiting for transfers between devices  85.7 us
    ppermute x16, starting transfers between devices, with_halo(): after = lax.ppermute(first, axis, down)  58.7 us
    ppermute x16, waiting for transfers between devices, with_halo(): before = lax.ppermute(last, axis, up)  55.6 us
    ppermute x16, starting transfers between devices, with_halo(): before = lax.ppermute(last, axis, up)  50 us
    all_gather x1, blocking collectives, local(): lax.all_gather(prestress, 'cross', axis=1, tiled=True)  28.7 us
    all_gather x1, blocking collectives, local(): lax.all_gather(rate_a, 'cross', axis=1, tiled=True)  28.3 us
    all_gather x1, blocking collectives, local(): lax.all_gather(normal_stress, 'cross', axis=1, tiled=True)  28.2 us
    ppermute x16, waiting for transfers between devices, with_halo(): after = lax.ppermute(first, axis, down)  27.3 us
  transfers between devices with their start and end apart: 35, of which 27 were waited for; matrix products, arithmetic and copies ran while one was open for 2% of the time, Pallas kernels for 0%

profile of v1, /device:TPU:32, one launch (start us, length us, event | category | flops | bytes accessed | tf_op | source)
XLA Modules:
  0.0 447.2 jit_solution(4799423150497831871)
XLA Ops:
  7.2 2.3 copy.50
  9.7 1.9 collective-permute-start
  11.6 6.0 %collective-permute-start.1 = (f32[6,2,16,256]{3,1,2,0:T(2,128)S(1)}, f32[6,2,16,256]{3,1,2,0:T(2,128)S(1)}, u32[]{:S(2)}, u32[]{:S(2)}) collective-permute-start(f32[6,2,16,256]{3,1,2,0:T(2,128)S(1)} %get-tuple-element.137), channel_id=1, source_target_pairs={{8,0},{16,8},{24,16},{32,24},{40,32},{48,40},{56,48},{64,56},{72,6... | collective-permute-start | bytes 589832 | tf_op jit(solution)/shard_map/ppermute | solution.py:23
  17.6 1.4 collective-permute-done
  19.0 1.8 collective-permute-done.1
  20.9 3.5 collective-permute-start.2
  24.4 1.3 collective-permute-start.3
  25.9 11.5 %collective-permute-done.2 = f32[6,20,2,256]{3,1,2,0:T(8,128)S(1)} collective-permute-done((f32[6,20,2,256]{3,1,2,0:T(8,128)S(1)}, f32[6,20,2,256]{3,1,2,0:T(8,128)S(1)}, u32[]{:S(2)}, u32[]{:S(2)}) %collective-permute-start.2) | collective-permute-done | bytes 245792 | tf_op jit(solution)/shard_map/ppermute | solution.py:22
  37.4 3.0 select_maximum_fusion.12
  44.1 2.7 collective-permute-start.4
  46.8 5.3 %collective-permute-start.5 = (f32[3,2,16,256]{3,1,2,0:T(2,128)S(1)}, f32[3,2,16,256]{3,1,2,0:T(2,128)S(1)}, u32[]{:S(2)}, u32[]{:S(2)}) collective-permute-start(f32[3,2,16,256]{3,1,2,0:T(2,128)S(1)} %get-tuple-element.157), channel_id=1, source_target_pairs={{8,0},{16,8},{24,16},{32,24},{40,32},{48,40},{56,48},{64,56},{72,6... | collective-permute-start | bytes 294920 | tf_op jit(solution)/shard_map/ppermute | solution.py:23
  52.4 1.8 collective-permute-done.5
  54.3 5.0 %collective-permute-start.6 = (f32[3,20,2,256]{3,1,2,0:T(8,128)S(1)}, f32[3,20,2,256]{3,1,2,0:T(8,128)}, u32[]{:S(2)}, u32[]{:S(2)}) collective-permute-start(f32[3,20,2,256]{3,1,2,0:T(8,128)S(1)} %get-tuple-element.148), channel_id=1, source_target_pairs={{0,1},{1,2},{2,3},{3,4},{4,5},{5,6},{6,7},{8,9},{9,10},{10,11},{11... | collective-permute-start | bytes 368648 | tf_op jit(solution)/shard_map/ppermute | solution.py:22
  61.4 7.1 %all-to-all-start = ((f32[8,1,512]{2,1,0:T(1,128)}), f32[8,1,512]{2,1,0:T(1,128)S(1)}, u32[]{:S(2)}, u32[]{:S(2)}) async-start(f32[8,1,512]{2,1,0:T(1,128)} %reshape.185), calls=%async_computation | async-start | bytes 32768 | tf_op jit(solution)/shard_map/all_to_all | solution.py:121
  68.6 28.7 %all-gather = f32[8,32,16]{1,2,0:T(8,128)S(1)} all-gather(f32[1,32,16]{1,2,0:T(8,128)S(1)} %bitcast.290), channel_id=1, replica_groups=mesh['strike'=32,'cross'=8] {'cross'}, dimensions={0}, use_global_device_ids=true | all-gather | bytes 18432 | tf_op jit(solution)/shard_map/all_gather | solution.py:117
  97.4 28.2 %all-gather.2 = f32[8,32,16]{1,2,0:T(8,128)S(1)} all-gather(f32[1,32,16]{1,2,0:T(8,128)S(1)} %bitcast.291), channel_id=1, replica_groups=mesh['strike'=32,'cross'=8] {'cross'}, dimensions={0}, use_global_device_ids=true | all-gather | bytes 18432 | tf_op jit(solution)/shard_map/all_gather | solution.py:118
  125.6 28.3 %all-gather.1 = f32[8,32,16]{1,2,0:T(8,128)S(1)} all-gather(f32[1,32,16]{1,2,0:T(8,128)S(1)} %bitcast.292), channel_id=1, replica_groups=mesh['strike'=32,'cross'=8] {'cross'}, dimensions={0}, use_global_device_ids=true | all-gather | bytes 18432 | tf_op jit(solution)/shard_map/all_gather | solution.py:119
  156.7 2.0 select_maximum_fusion.28
  164.5 1.9 collective-permute-start.8
  166.4 6.0 %collective-permute-start.9 = (f32[6,2,16,256]{3,1,2,0:T(2,128)S(1)}, f32[6,2,16,256]{3,1,2,0:T(2,128)S(1)}, u32[]{:S(2)}, u32[]{:S(2)}) collective-permute-start(f32[6,2,16,256]{3,1,2,0:T(2,128)S(1)} %get-tuple-element.135), channel_id=1, source_target_pairs={{8,0},{16,8},{24,16},{32,24},{40,32},{48,40},{56,48},{64,56},{72,6... | collective-permute-start | bytes 589832 | tf_op jit(solution)/shard_map/ppermute | solution.py:23
  172.5 1.4 collective-permute-done.8
  173.9 1.8 collective-permute-done.9
  175.8 3.4 collective-permute-start.10
  180.4 11.6 %collective-permute-done.10 = f32[6,20,2,256]{3,1,2,0:T(8,128)S(1)} collective-permute-done((f32[6,20,2,256]{3,1,2,0:T(8,128)S(1)}, f32[6,20,2,256]{3,1,2,0:T(8,128)S(1)}, u32[]{:S(2)}, u32[]{:S(2)}) %collective-permute-start.10) | collective-permute-done | bytes 245792 | tf_op jit(solution)/shard_map/ppermute | solution.py:22
  192.0 3.0 select_maximum_fusion.8
  198.5 1.9 collective-permute-start.12
  200.5 6.0 %collective-permute-start.13 = (f32[3,2,16,256]{3,1,2,0:T(2,128)S(1)}, f32[3,2,16,256]{3,1,2,0:T(2,128)S(1)}, u32[]{:S(2)}, u32[]{:S(2)}) collective-permute-start(f32[3,2,16,256]{3,1,2,0:T(2,128)S(1)} %get-tuple-element.155), channel_id=1, source_target_pairs={{8,0},{16,8},{24,16},{32,24},{40,32},{48,40},{56,48},{64,56},{72,6... | collective-permute-start | bytes 294920 | tf_op jit(solution)/shard_map/ppermute | solution.py:23
  206.9 1.8 collective-permute-done.13
  208.8 4.4 collective-permute-start.14
  213.2 1.5 collective-permute-start.15
  215.8 4.4 collective-permute-done.15
  225.0 1.9 collective-permute-start.16
  226.9 6.0 %collective-permute-start.17 = (f32[6,2,16,256]{3,1,2,0:T(2,128)S(1)}, f32[6,2,16,256]{3,1,2,0:T(2,128)S(1)}, u32[]{:S(2)}, u32[]{:S(2)}) collective-permute-start(f32[6,2,16,256]{3,1,2,0:T(2,128)S(1)} %get-tuple-element.133), channel_id=1, source_target_pairs={{8,0},{16,8},{24,16},{32,24},{40,32},{48,40},{56,48},{64,56},{72,6... | collective-permute-start | bytes 589832 | tf_op jit(solution)/shard_map/ppermute | solution.py:23
  233.0 1.4 collective-permute-done.16
  234.4 1.8 collective-permute-done.17
  236.3 4.0 collective-permute-start.18
  240.3 1.3 collective-permute-start.19
  241.6 11.6 %collective-permute-done.18 = f32[6,20,2,256]{3,1,2,0:T(8,128)S(1)} collective-permute-done((f32[6,20,2,256]{3,1,2,0:T(8,128)S(1)}, f32[6,20,2,256]{3,1,2,0:T(8,128)S(1)}, u32[]{:S(2)}, u32[]{:S(2)}) %collective-permute-start.18) | collective-permute-done | bytes 245792 | tf_op jit(solution)/shard_map/ppermute | solution.py:22
  253.1 3.0 select_maximum_fusion.4
  259.7 1.9 collective-permute-start.20
  261.6 6.0 %collective-permute-start.21 = (f32[3,2,16,256]{3,1,2,0:T(2,128)S(1)}, f32[3,2,16,256]{3,1,2,0:T(2,128)S(1)}, u32[]{:S(2)}, u32[]{:S(2)}) collective-permute-start(f32[3,2,16,256]{3,1,2,0:T(2,128)S(1)} %get-tuple-element.153), channel_id=1, source_target_pairs={{8,0},{16,8},{24,16},{32,24},{40,32},{48,40},{56,48},{64,56},{72,6... | collective-permute-start | bytes 294920 | tf_op jit(solution)/shard_map/ppermute | solution.py:23
  268.1 1.8 collective-permute-done.21
  269.9 4.4 collective-permute-start.22
  274.3 1.7 collective-permute-start.23
  276.9 4.4 collective-permute-done.23
  286.1 1.9 collective-permute-start.24
  288.1 6.0 %collective-permute-start.25 = (f32[6,2,16,256]{3,1,2,0:T(2,128)S(1)}, f32[6,2,16,256]{3,1,2,0:T(2,128)S(1)}, u32[]{:S(2)}, u32[]{:S(2)}) collective-permute-start(f32[6,2,16,256]{3,1,2,0:T(2,128)S(1)} %get-tuple-element.131), channel_id=1, source_target_pairs={{8,0},{16,8},{24,16},{32,24},{40,32},{48,40},{56,48},{64,56},{72,6... | collective-permute-start | bytes 589832 | tf_op jit(solution)/shard_map/ppermute | solution.py:23
  294.1 1.4 collective-permute-done.24
  295.5 1.8 collective-permute-done.25
  297.4 4.8 %collective-permute-start.26 = (f32[6,20,2,256]{3,1,2,0:T(8,128)S(1)}, f32[6,20,2,256]{3,1,2,0:T(8,128)S(1)}, u32[]{:S(2)}, u32[]{:S(2)}) collective-permute-start(f32[6,20,2,256]{3,1,2,0:T(8,128)S(1)} %get-tuple-element.122), channel_id=1, source_target_pairs={{0,1},{1,2},{2,3},{3,4},{4,5},{5,6},{6,7},{8,9},{9,10},{10,11},{11... | collective-permute-start | bytes 737288 | tf_op jit(solution)/shard_map/ppermute | solution.py:22
  303.5 11.6 %collective-permute-done.26 = f32[6,20,2,256]{3,1,2,0:T(8,128)S(1)} collective-permute-done((f32[6,20,2,256]{3,1,2,0:T(8,128)S(1)}, f32[6,20,2,256]{3,1,2,0:T(8,128)S(1)}, u32[]{:S(2)}, u32[]{:S(2)}) %collective-permute-start.26) | collective-permute-done | bytes 245792 | tf_op jit(solution)/shard_map/ppermute | solution.py:22
  315.1 3.0 select_maximum_fusion
  321.8 1.9 collective-permute-start.28
  323.7 6.0 %collective-permute-start.29 = (f32[3,2,16,256]{3,1,2,0:T(2,128)S(1)}, f32[3,2,16,256]{3,1,2,0:T(2,128)S(1)}, u32[]{:S(2)}, u32[]{:S(2)}) collective-permute-start(f32[3,2,16,256]{3,1,2,0:T(2,128)S(1)} %get-tuple-element.151), channel_id=1, source_target_pairs={{8,0},{16,8},{24,16},{32,24},{40,32},{48,40},{56,48},{64,56},{72,6... | collective-permute-start | bytes 294920 | tf_op jit(solution)/shard_map/ppermute | solution.py:23
  330.2 1.8 collective-permute-done.29
  332.0 4.4 collective-permute-start.30
  336.4 1.5 collective-permute-start.31
  337.9 1.3 copy.67
  339.2 4.2 collective-permute-done.31
  349.7 2.0 copy.68
  351.7 46.3 %reduce-scatter.7.cloned.1.call-done = f32[32,16]{1,0:T(8,128)} async-done(((f32[256,16]{1,0:T(8,128)}), f32[32,16]{1,0:T(8,128)}) %reduce-scatter.7.cloned.1.call-update) | async-done | bytes 2064
  398.1 1.4 copy.70
  399.5 39.4 %reduce-scatter.9.cloned.1.call-done = f32[32,16]{1,0:T(8,128)} async-done(((f32[256,16]{1,0:T(8,128)}), f32[32,16]{1,0:T(8,128)}) %reduce-scatter.9.cloned.1.call-update) | async-done | bytes 2064
  438.8 1.4 copy.72
  (140 shorter events, 47.1 us)
Async XLA Ops:
  9.5 16.2 %copy-start.4 = (f32[16,16,256]{2,1,0:T(8,128)S(1)}, f32[16,16,256]{2,1,0:T(8,128)}, u32[]{:S(2)}) copy-start(f32[16,16,256]{2,1,0:T(8,128)} %param.20) | copy-start | bytes 786436
  9.7 9.4 %collective-permute-start = (f32[6,2,16,256]{3,1,2,0:T(2,128)S(1)}, f32[6,2,16,256]{3,1,2,0:T(2,128)S(1)}, u32[]{:S(2)}, u32[]{:S(2)}) collective-permute-start(f32[6,2,16,256]{3,1,2,0:T(2,128)S(1)} %get-tuple-element.136), channel_id=1, source_target_pairs={{0,8},{8,16},{16,24},{24,32},{32,40},{40,48},{48,56},{56,64},{64,7... | collective-permute-start | bytes 589832 | tf_op jit(solution)/shard_map/ppermute | solution.py:22
  11.6 9.2 %collective-permute-start.1 = (f32[6,2,16,256]{3,1,2,0:T(2,128)S(1)}, f32[6,2,16,256]{3,1,2,0:T(2,128)S(1)}, u32[]{:S(2)}, u32[]{:S(2)}) collective-permute-start(f32[6,2,16,256]{3,1,2,0:T(2,128)S(1)} %get-tuple-element.137), channel_id=1, source_target_pairs={{8,0},{16,8},{24,16},{32,24},{40,32},{48,40},{56,48},{64,56},{72,6... | collective-permute-start | bytes 589832 | tf_op jit(solution)/shard_map/ppermute | solution.py:23
  20.9 16.5 %collective-permute-start.2 = (f32[6,20,2,256]{3,1,2,0:T(8,128)S(1)}, f32[6,20,2,256]{3,1,2,0:T(8,128)S(1)}, u32[]{:S(2)}, u32[]{:S(2)}) collective-permute-start(f32[6,20,2,256]{3,1,2,0:T(8,128)S(1)} %get-tuple-element.128), channel_id=1, source_target_pairs={{0,1},{1,2},{2,3},{3,4},{4,5},{5,6},{6,7},{8,9},{9,10},{10,11},{11... | collective-permute-start | bytes 737288 | tf_op jit(solution)/shard_map/ppermute | solution.py:22
  24.4 13.0 %collective-permute-start.3 = (f32[6,20,2,256]{3,1,2,0:T(8,128)S(1)}, f32[6,20,2,256]{3,1,2,0:T(8,128)S(1)}, u32[]{:S(2)}, u32[]{:S(2)}) collective-permute-start(f32[6,20,2,256]{3,1,2,0:T(8,128)S(1)} %get-tuple-element.129), channel_id=1, source_target_pairs={{1,0},{2,1},{3,2},{4,3},{5,4},{6,5},{7,6},{9,8},{10,9},{11,10},{12... | collective-permute-start | bytes 737288 | tf_op jit(solution)/shard_map/ppermute | solution.py:23
  42.3 1.1 copy-start.1
  43.5 17.2 %copy-start.5 = (f32[16,32]{1,0:T(8,128)S(1)}, f32[16,32]{1,0:T(8,128)}, u32[]{:S(2)}) copy-start(f32[16,32]{1,0:T(8,128)} %param.27) | copy-start | bytes 6148
  43.5 25.1 %copy-start.6 = (f32[16,32]{1,0:T(8,128)S(1)}, f32[16,32]{1,0:T(8,128)}, u32[]{:S(2)}) copy-start(f32[16,32]{1,0:T(8,128)} %param.24) | copy-start | bytes 6148
  43.5 53.9 %copy-start.7 = (f32[16,32]{1,0:T(8,128)S(1)}, f32[16,32]{1,0:T(8,128)}, u32[]{:S(2)}) copy-start(f32[16,32]{1,0:T(8,128)} %param.25) | copy-start | bytes 6148
  43.5 82.2 %copy-start.8 = (f32[16,32]{1,0:T(8,128)S(1)}, f32[16,32]{1,0:T(8,128)}, u32[]{:S(2)}) copy-start(f32[16,32]{1,0:T(8,128)} %param.26) | copy-start | bytes 6148
  43.5 110.6 %copy-start.9 = (s32[32]{0:T(128)S(1)}, s32[32]{0:T(128)}, u32[]{:S(2)}) copy-start(s32[32]{0:T(128)} %param.23) | copy-start | bytes 388
  44.1 8.3 %collective-permute-start.4 = (f32[3,2,16,256]{3,1,2,0:T(2,128)S(1)}, f32[3,2,16,256]{3,1,2,0:T(2,128)S(1)}, u32[]{:S(2)}, u32[]{:S(2)}) collective-permute-start(f32[3,2,16,256]{3,1,2,0:T(2,128)S(1)} %get-tuple-element.156), channel_id=1, source_target_pairs={{0,8},{8,16},{16,24},{24,32},{32,40},{40,48},{48,56},{56,64},{64,7... | collective-permute-start | bytes 294920 | tf_op jit(solution)/shard_map/ppermute | solution.py:22
  46.8 7.5 %collective-permute-start.5 = (f32[3,2,16,256]{3,1,2,0:T(2,128)S(1)}, f32[3,2,16,256]{3,1,2,0:T(2,128)S(1)}, u32[]{:S(2)}, u32[]{:S(2)}) collective-permute-start(f32[3,2,16,256]{3,1,2,0:T(2,128)S(1)} %get-tuple-element.157), channel_id=1, source_target_pairs={{8,0},{16,8},{24,16},{32,24},{40,32},{48,40},{56,48},{64,56},{72,6... | collective-permute-start | bytes 294920 | tf_op jit(solution)/shard_map/ppermute | solution.py:23
  54.3 102.4 %collective-permute-start.6 = (f32[3,20,2,256]{3,1,2,0:T(8,128)S(1)}, f32[3,20,2,256]{3,1,2,0:T(8,128)}, u32[]{:S(2)}, u32[]{:S(2)}) collective-permute-start(f32[3,20,2,256]{3,1,2,0:T(8,128)S(1)} %get-tuple-element.148), channel_id=1, source_target_pairs={{0,1},{1,2},{2,3},{3,4},{4,5},{5,6},{6,7},{8,9},{9,10},{10,11},{11... | collective-permute-start | bytes 368648 | tf_op jit(solution)/shard_map/ppermute | solution.py:22
  59.4 97.4 %collective-permute-start.7 = (f32[3,20,2,256]{3,1,2,0:T(8,128)S(1)}, f32[3,20,2,256]{3,1,2,0:T(8,128)}, u32[]{:S(2)}, u32[]{:S(2)}) collective-permute-start(f32[3,20,2,256]{3,1,2,0:T(8,128)S(1)} %get-tuple-element.149), channel_id=1, source_target_pairs={{1,0},{2,1},{3,2},{4,3},{5,4},{6,5},{7,6},{9,8},{10,9},{11,10},{12... | collective-permute-start | bytes 368648 | tf_op jit(solution)/shard_map/ppermute | solution.py:23
  61.4 94.0 %all-to-all-start = ((f32[8,1,512]{2,1,0:T(1,128)}), f32[8,1,512]{2,1,0:T(1,128)S(1)}, u32[]{:S(2)}, u32[]{:S(2)}) async-start(f32[8,1,512]{2,1,0:T(1,128)} %reshape.185), calls=%async_computation | async-start | bytes 32768 | tf_op jit(solution)/shard_map/all_to_all | solution.py:121
  68.5 329.6 %reduce-scatter.7.cloned.1.call-start = ((), (), s32[]{:S(2)}) async-start(), calls=%async_computation.3 | async-start | bytes 147456
  159.5 1.0 copy-start
  159.6 1.0 copy-start.3
  161.5 1.4 copy-start.2
  164.5 9.4 %collective-permute-start.8 = (f32[6,2,16,256]{3,1,2,0:T(2,128)S(1)}, f32[6,2,16,256]{3,1,2,0:T(2,128)S(1)}, u32[]{:S(2)}, u32[]{:S(2)}) collective-permute-start(f32[6,2,16,256]{3,1,2,0:T(2,128)S(1)} %get-tuple-element.134), channel_id=1, source_target_pairs={{0,8},{8,16},{16,24},{24,32},{32,40},{40,48},{48,56},{56,64},{64,7... | collective-permute-start | bytes 589832 | tf_op jit(solution)/shard_map/ppermute | solution.py:22
  166.4 9.3 %collective-permute-start.9 = (f32[6,2,16,256]{3,1,2,0:T(2,128)S(1)}, f32[6,2,16,256]{3,1,2,0:T(2,128)S(1)}, u32[]{:S(2)}, u32[]{:S(2)}) collective-permute-start(f32[6,2,16,256]{3,1,2,0:T(2,128)S(1)} %get-tuple-element.135), channel_id=1, source_target_pairs={{8,0},{16,8},{24,16},{32,24},{40,32},{48,40},{56,48},{64,56},{72,6... | collective-permute-start | bytes 589832 | tf_op jit(solution)/shard_map/ppermute | solution.py:23
  175.8 16.2 %collective-permute-start.10 = (f32[6,20,2,256]{3,1,2,0:T(8,128)S(1)}, f32[6,20,2,256]{3,1,2,0:T(8,128)S(1)}, u32[]{:S(2)}, u32[]{:S(2)}) collective-permute-start(f32[6,20,2,256]{3,1,2,0:T(8,128)S(1)} %get-tuple-element.126), channel_id=1, source_target_pairs={{0,1},{1,2},{2,3},{3,4},{4,5},{5,6},{6,7},{8,9},{9,10},{10,11},{11... | collective-permute-start | bytes 737288 | tf_op jit(solution)/shard_map/ppermute | solution.py:22
  179.1 12.9 %collective-permute-start.11 = (f32[6,20,2,256]{3,1,2,0:T(8,128)S(1)}, f32[6,20,2,256]{3,1,2,0:T(8,128)S(1)}, u32[]{:S(2)}, u32[]{:S(2)}) collective-permute-start(f32[6,20,2,256]{3,1,2,0:T(8,128)S(1)} %get-tuple-element.127), channel_id=1, source_target_pairs={{1,0},{2,1},{3,2},{4,3},{5,4},{6,5},{7,6},{9,8},{10,9},{11,10},{12... | collective-permute-start | bytes 737288 | tf_op jit(solution)/shard_map/ppermute | solution.py:23
  198.5 8.4 %collective-permute-start.12 = (f32[3,2,16,256]{3,1,2,0:T(2,128)S(1)}, f32[3,2,16,256]{3,1,2,0:T(2,128)S(1)}, u32[]{:S(2)}, u32[]{:S(2)}) collective-permute-start(f32[3,2,16,256]{3,1,2,0:T(2,128)S(1)} %get-tuple-element.154), channel_id=1, source_target_pairs={{0,8},{8,16},{16,24},{24,32},{32,40},{40,48},{48,56},{56,64},{64,7... | collective-permute-start | bytes 294920 | tf_op jit(solution)/shard_map/ppermute | solution.py:22
  200.5 8.2 %collective-permute-start.13 = (f32[3,2,16,256]{3,1,2,0:T(2,128)S(1)}, f32[3,2,16,256]{3,1,2,0:T(2,128)S(1)}, u32[]{:S(2)}, u32[]{:S(2)}) collective-permute-start(f32[3,2,16,256]{3,1,2,0:T(2,128)S(1)} %get-tuple-element.155), channel_id=1, source_target_pairs={{8,0},{16,8},{24,16},{32,24},{40,32},{48,40},{56,48},{64,56},{72,6... | collective-permute-start | bytes 294920 | tf_op jit(solution)/shard_map/ppermute | solution.py:23
  208.8 7.1 %collective-permute-start.14 = (f32[3,20,2,256]{3,1,2,0:T(8,128)S(1)}, f32[3,20,2,256]{3,1,2,0:T(8,128)S(1)}, u32[]{:S(2)}, u32[]{:S(2)}) collective-permute-start(f32[3,20,2,256]{3,1,2,0:T(8,128)S(1)} %get-tuple-element.146), channel_id=1, source_target_pairs={{0,1},{1,2},{2,3},{3,4},{4,5},{5,6},{6,7},{8,9},{9,10},{10,11},{11... | collective-permute-start | bytes 368648 | tf_op jit(solution)/shard_map/ppermute | solution.py:22
  213.2 7.0 %collective-permute-start.15 = (f32[3,20,2,256]{3,1,2,0:T(8,128)S(1)}, f32[3,20,2,256]{3,1,2,0:T(8,128)S(1)}, u32[]{:S(2)}, u32[]{:S(2)}) collective-permute-start(f32[3,20,2,256]{3,1,2,0:T(8,128)S(1)} %get-tuple-element.147), channel_id=1, source_target_pairs={{1,0},{2,1},{3,2},{4,3},{5,4},{6,5},{7,6},{9,8},{10,9},{11,10},{12... | collective-permute-start | bytes 368648 | tf_op jit(solution)/shard_map/ppermute | solution.py:23
  225.0 9.4 %collective-permute-start.16 = (f32[6,2,16,256]{3,1,2,0:T(2,128)S(1)}, f32[6,2,16,256]{3,1,2,0:T(2,128)S(1)}, u32[]{:S(2)}, u32[]{:S(2)}) collective-permute-start(f32[6,2,16,256]{3,1,2,0:T(2,128)S(1)} %get-tuple-element.132), channel_id=1, source_target_pairs={{0,8},{8,16},{16,24},{24,32},{32,40},{40,48},{48,56},{56,64},{64,7... | collective-permute-start | bytes 589832 | tf_op jit(solution)/shard_map/ppermute | solution.py:22
  226.9 9.3 %collective-permute-start.17 = (f32[6,2,16,256]{3,1,2,0:T(2,128)S(1)}, f32[6,2,16,256]{3,1,2,0:T(2,128)S(1)}, u32[]{:S(2)}, u32[]{:S(2)}) collective-permute-start(f32[6,2,16,256]{3,1,2,0:T(2,128)S(1)} %get-tuple-element.133), channel_id=1, source_target_pairs={{8,0},{16,8},{24,16},{32,24},{40,32},{48,40},{56,48},{64,56},{72,6... | collective-permute-start | bytes 589832 | tf_op jit(solution)/shard_map/ppermute | solution.py:23
  236.3 16.9 %collective-permute-start.18 = (f32[6,20,2,256]{3,1,2,0:T(8,128)S(1)}, f32[6,20,2,256]{3,1,2,0:T(8,128)S(1)}, u32[]{:S(2)}, u32[]{:S(2)}) collective-permute-start(f32[6,20,2,256]{3,1,2,0:T(8,128)S(1)} %get-tuple-element.124), channel_id=1, source_target_pairs={{0,1},{1,2},{2,3},{3,4},{4,5},{5,6},{6,7},{8,9},{9,10},{10,11},{11... | collective-permute-start | bytes 737288 | tf_op jit(solution)/shard_map/ppermute | solution.py:22
  240.3 12.9 %collective-permute-start.19 = (f32[6,20,2,256]{3,1,2,0:T(8,128)S(1)}, f32[6,20,2,256]{3,1,2,0:T(8,128)S(1)}, u32[]{:S(2)}, u32[]{:S(2)}) collective-permute-start(f32[6,20,2,256]{3,1,2,0:T(8,128)S(1)} %get-tuple-element.125), channel_id=1, source_target_pairs={{1,0},{2,1},{3,2},{4,3},{5,4},{6,5},{7,6},{9,8},{10,9},{11,10},{12... | collective-permute-start | bytes 737288 | tf_op jit(solution)/shard_map/ppermute | solution.py:23
  259.7 8.4 %collective-permute-start.20 = (f32[3,2,16,256]{3,1,2,0:T(2,128)S(1)}, f32[3,2,16,256]{3,1,2,0:T(2,128)S(1)}, u32[]{:S(2)}, u32[]{:S(2)}) collective-permute-start(f32[3,2,16,256]{3,1,2,0:T(2,128)S(1)} %get-tuple-element.152), channel_id=1, source_target_pairs={{0,8},{8,16},{16,24},{24,32},{32,40},{40,48},{48,56},{56,64},{64,7... | collective-permute-start | bytes 294920 | tf_op jit(solution)/shard_map/ppermute | solution.py:22
  261.6 8.2 %collective-permute-start.21 = (f32[3,2,16,256]{3,1,2,0:T(2,128)S(1)}, f32[3,2,16,256]{3,1,2,0:T(2,128)S(1)}, u32[]{:S(2)}, u32[]{:S(2)}) collective-permute-start(f32[3,2,16,256]{3,1,2,0:T(2,128)S(1)} %get-tuple-element.153), channel_id=1, source_target_pairs={{8,0},{16,8},{24,16},{32,24},{40,32},{48,40},{56,48},{64,56},{72,6... | collective-permute-start | bytes 294920 | tf_op jit(solution)/shard_map/ppermute | solution.py:23
  269.9 7.1 %collective-permute-start.22 = (f32[3,20,2,256]{3,1,2,0:T(8,128)S(1)}, f32[3,20,2,256]{3,1,2,0:T(8,128)S(1)}, u32[]{:S(2)}, u32[]{:S(2)}) collective-permute-start(f32[3,20,2,256]{3,1,2,0:T(8,128)S(1)} %get-tuple-element.144), channel_id=1, source_target_pairs={{0,1},{1,2},{2,3},{3,4},{4,5},{5,6},{6,7},{8,9},{9,10},{10,11},{11... | collective-permute-start | bytes 368648 | tf_op jit(solution)/shard_map/ppermute | solution.py:22
  274.3 7.0 %collective-permute-start.23 = (f32[3,20,2,256]{3,1,2,0:T(8,128)S(1)}, f32[3,20,2,256]{3,1,2,0:T(8,128)S(1)}, u32[]{:S(2)}, u32[]{:S(2)}) collective-permute-start(f32[3,20,2,256]{3,1,2,0:T(8,128)S(1)} %get-tuple-element.145), channel_id=1, source_target_pairs={{1,0},{2,1},{3,2},{4,3},{5,4},{6,5},{7,6},{9,8},{10,9},{11,10},{12... | collective-permute-start | bytes 368648 | tf_op jit(solution)/shard_map/ppermute | solution.py:23
  286.1 9.4 %collective-permute-start.24 = (f32[6,2,16,256]{3,1,2,0:T(2,128)S(1)}, f32[6,2,16,256]{3,1,2,0:T(2,128)S(1)}, u32[]{:S(2)}, u32[]{:S(2)}) collective-permute-start(f32[6,2,16,256]{3,1,2,0:T(2,128)S(1)} %get-tuple-element.130), channel_id=1, source_target_pairs={{0,8},{8,16},{16,24},{24,32},{32,40},{40,48},{48,56},{56,64},{64,7... | collective-permute-start | bytes 589832 | tf_op jit(solution)/shard_map/ppermute | solution.py:22
  288.1 9.3 %collective-permute-start.25 = (f32[6,2,16,256]{3,1,2,0:T(2,128)S(1)}, f32[6,2,16,256]{3,1,2,0:T(2,128)S(1)}, u32[]{:S(2)}, u32[]{:S(2)}) collective-permute-start(f32[6,2,16,256]{3,1,2,0:T(2,128)S(1)} %get-tuple-element.131), channel_id=1, source_target_pairs={{8,0},{16,8},{24,16},{32,24},{40,32},{48,40},{56,48},{64,56},{72,6... | collective-permute-start | bytes 589832 | tf_op jit(solution)/shard_map/ppermute | solution.py:23
  297.4 17.7 %collective-permute-start.26 = (f32[6,20,2,256]{3,1,2,0:T(8,128)S(1)}, f32[6,20,2,256]{3,1,2,0:T(8,128)S(1)}, u32[]{:S(2)}, u32[]{:S(2)}) collective-permute-start(f32[6,20,2,256]{3,1,2,0:T(8,128)S(1)} %get-tuple-element.122), channel_id=1, source_target_pairs={{0,1},{1,2},{2,3},{3,4},{4,5},{5,6},{6,7},{8,9},{9,10},{10,11},{11... | collective-permute-start | bytes 737288 | tf_op jit(solution)/shard_map/ppermute | solution.py:22
  302.2 12.9 %collective-permute-start.27 = (f32[6,20,2,256]{3,1,2,0:T(8,128)S(1)}, f32[6,20,2,256]{3,1,2,0:T(8,128)S(1)}, u32[]{:S(2)}, u32[]{:S(2)}) collective-permute-start(f32[6,20,2,256]{3,1,2,0:T(8,128)S(1)} %get-tuple-element.123), channel_id=1, source_target_pairs={{1,0},{2,1},{3,2},{4,3},{5,4},{6,5},{7,6},{9,8},{10,9},{11,10},{12... | collective-permute-start | bytes 737288 | tf_op jit(solution)/shard_map/ppermute | solution.py:23
  321.8 8.4 %collective-permute-start.28 = (f32[3,2,16,256]{3,1,2,0:T(2,128)S(1)}, f32[3,2,16,256]{3,1,2,0:T(2,128)S(1)}, u32[]{:S(2)}, u32[]{:S(2)}) collective-permute-start(f32[3,2,16,256]{3,1,2,0:T(2,128)S(1)} %get-tuple-element.150), channel_id=1, source_target_pairs={{0,8},{8,16},{16,24},{24,32},{32,40},{40,48},{48,56},{56,64},{64,7... | collective-permute-start | bytes 294920 | tf_op jit(solution)/shard_map/ppermute | solution.py:22
  323.7 8.2 %collective-permute-start.29 = (f32[3,2,16,256]{3,1,2,0:T(2,128)S(1)}, f32[3,2,16,256]{3,1,2,0:T(2,128)S(1)}, u32[]{:S(2)}, u32[]{:S(2)}) collective-permute-start(f32[3,2,16,256]{3,1,2,0:T(2,128)S(1)} %get-tuple-element.151), channel_id=1, source_target_pairs={{8,0},{16,8},{24,16},{32,24},{40,32},{48,40},{56,48},{64,56},{72,6... | collective-permute-start | bytes 294920 | tf_op jit(solution)/shard_map/ppermute | solution.py:23
  332.0 7.2 %collective-permute-start.30 = (f32[3,20,2,256]{3,1,2,0:T(8,128)S(1)}, f32[3,20,2,256]{3,1,2,0:T(8,128)S(1)}, u32[]{:S(2)}, u32[]{:S(2)}) collective-permute-start(f32[3,20,2,256]{3,1,2,0:T(8,128)S(1)} %get-tuple-element.142), channel_id=1, source_target_pairs={{0,1},{1,2},{2,3},{3,4},{4,5},{5,6},{6,7},{8,9},{9,10},{10,11},{11... | collective-permute-start | bytes 368648 | tf_op jit(solution)/shard_map/ppermute | solution.py:22
  336.4 7.0 %collective-permute-start.31 = (f32[3,20,2,256]{3,1,2,0:T(8,128)S(1)}, f32[3,20,2,256]{3,1,2,0:T(8,128)S(1)}, u32[]{:S(2)}, u32[]{:S(2)}) collective-permute-start(f32[3,20,2,256]{3,1,2,0:T(8,128)S(1)} %get-tuple-element.143), channel_id=1, source_target_pairs={{1,0},{2,1},{3,2},{4,3},{5,4},{6,5},{7,6},{9,8},{10,9},{11,10},{12... | collective-permute-start | bytes 368648 | tf_op jit(solution)/shard_map/ppermute | solution.py:23
  348.8 90.0 %reduce-scatter.9.cloned.1.call-start = ((), (), s32[]{:S(2)}) async-start(), calls=%async_computation.4 | async-start | bytes 147456
Sparse Core Ops, SparseCore 0:
  348.9 49.0 reduce-scatter.6
  400.7 38.0 reduce-scatter.8
